TPU v7x, 128 devices: a whole 4x4x4 slice. The times are simulated.
128 devices in a mesh: row: 8 (over z, x_hi), col: 16 (over x_lo, y, core).
Axes of the slice: x: 4 (x_hi: 2, x_lo: 2; x = x_hi * 2 + x_lo), y: 4, z: 4, core: 2. Of those that a mesh axis runs over, the one named last changes fastest.
Arguments:
- pair: bfloat16 [1024, 1024, 128], P('row', 'col'), may hold values from -6 to 6
- left_gate: bfloat16 [128, 128], replicated, may hold values from -0.5 to 0.5
- left_proj: bfloat16 [128, 128], replicated, may hold values from -0.5 to 0.5
- right_gate: bfloat16 [128, 128], replicated, may hold values from -0.5 to 0.5
- right_proj: bfloat16 [128, 128], replicated, may hold values from -0.5 to 0.5
- out_gate: bfloat16 [128, 128], replicated, may hold values from -0.5 to 0.5
- out_proj: bfloat16 [128, 128], replicated, may hold values from -0.5 to 0.5
Outputs:
- update: bfloat16 [1024, 1024, 128], P('row', 'col')
All inputs are finite; a program needn't handle non-finite values.
Results may differ from a plain program's by a relative error of at most 0.0078.
Values may be sent and summed in bfloat16 or wider, within the bound.
No kernel may reach another device: no remote copies, remote signals or barrier semaphores. Data moves between devices by JAX's collectives and lax.ppermute only.
A program may use at most 192 MiB of HBM per device.

v0:
```python
import jax
import jax.numpy as jnp
from jax import lax
from jax.experimental import pallas as pl
from jax.experimental.pallas import tpu as pltpu
from jax.sharding import PartitionSpec as P

C = 128
F32 = jnp.float32
BF16 = jnp.bfloat16
BLOCK = 16
PITCH = BLOCK + 1
VMEM = 24 * 1024 * 1024
FULL = 63 * 1024 * 1024

NT = (((1,), (1,)), ((), ()))
TN = (((0,), (0,)), ((), ()))


def norm_rows(x):
    x = x.astype(F32)
    center = x - jnp.mean(x, axis=-1, keepdims=True)
    spread = jnp.mean(center * center, axis=-1, keepdims=True)
    return (center * lax.rsqrt(spread + 1e-05)).astype(BF16)


def edges_kernel(
    x_hbm, lg_hbm, lp_hbm, rg_hbm, rp_hbm, og_hbm, o_hbm, g_hbm,
    x_ref, o_ref, g_ref, w_in, w_ref, stage_l, stage_r, x_sem, o_sem, g_sem, w_sem
):
    weights = [
        pltpu.make_async_copy(ref, w_in.at[n], w_sem.at[n])
        for n, ref in enumerate((lg_hbm, lp_hbm, rg_hbm, rp_hbm, og_hbm))
    ]
    parts = x_sem.shape[0]
    part = x_ref.shape[1] // parts
    loads = [
        pltpu.make_async_copy(
            x_hbm.at[:, pl.ds(n * part, part)], x_ref.at[:, pl.ds(n * part, part)], x_sem.at[n]
        )
        for n in range(parts)
    ]
    for copy in weights + loads:
        copy.start()
    for n, copy in enumerate(weights):
        copy.wait()
        if n < 4:
            w_ref[n * C : (n + 1) * C, :] = w_in[n].T * 0.5
        else:
            w_in[n] = w_in[n] * 0.5

    stores = []
    for n, copy in enumerate(loads):
        copy.wait()
        first = n * part
        for s in range(0, part, 2):
            x = jnp.concatenate(
                [x_ref[0, first + s], x_ref[1, first + s]]
                + [x_ref[0, first + s + 1], x_ref[1, first + s + 1]],
                axis=0,
            )
            x = norm_rows(x)
            q = jnp.dot(x, w_in[4], preferred_element_type=F32)
            q = (jnp.tanh(q) * 0.5 + 0.5).astype(BF16).reshape(2, 2, -1, C)
            g_ref[0, first + s], g_ref[1, first + s] = q[0, 0], q[0, 1]
            g_ref[0, first + s + 1], g_ref[1, first + s + 1] = q[1, 0], q[1, 1]
            p = lax.dot_general(w_ref[...], x, NT, preferred_element_type=F32)
            for side, stage in enumerate((stage_l, stage_r)):
                at = 2 * C * side
                half = p[at + C : at + 2 * C]
                edge = jnp.tanh(p[at : at + C]) * half + half
                stage[pl.ds(s, C, stride=PITCH), :] = edge[:, :C]
                stage[pl.ds(s + 1, C, stride=PITCH), :] = edge[:, C:]
        for side, stage in enumerate((stage_l, stage_r)):
            for c in range(C):
                o_ref[c, side, first : first + part, :] = stage[
                    c * PITCH : c * PITCH + part, :
                ].astype(BF16)
        at = pl.ds(first, part)
        for store in (
            pltpu.make_async_copy(o_ref.at[:, :, at], o_hbm.at[:, :, at], o_sem.at[n]),
            pltpu.make_async_copy(g_ref.at[:, at], g_hbm.at[:, at], g_sem.at[n]),
        ):
            store.start()
            stores.append(store)
    for store in stores:
        store.wait()


def edges(pair4, lg, lp, rg, rp, og):
    _, steps, cols, ch = pair4.shape
    parts = steps // BLOCK
    hbm = pl.BlockSpec(memory_space=pltpu.HBM)
    stage = pltpu.VMEM((C * PITCH, 2 * cols), F32)
    return pl.pallas_call(
        edges_kernel,
        in_specs=[hbm] * 6,
        out_specs=[hbm, hbm],
        out_shape=[
            jax.ShapeDtypeStruct((C, 2, steps, 2 * cols), BF16),
            jax.ShapeDtypeStruct(pair4.shape, BF16),
        ],
        scratch_shapes=[
            pltpu.VMEM(pair4.shape, BF16),
            pltpu.VMEM((C, 2, steps, 2 * cols), BF16),
            pltpu.VMEM(pair4.shape, BF16),
            pltpu.VMEM((5, C, C), BF16),
            pltpu.VMEM((4 * C, C), BF16),
            stage,
            stage,
            pltpu.SemaphoreType.DMA((parts,)),
            pltpu.SemaphoreType.DMA((parts,)),
            pltpu.SemaphoreType.DMA((parts,)),
            pltpu.SemaphoreType.DMA((5,)),
        ],
        compiler_params=pltpu.CompilerParams(vmem_limit_bytes=FULL),
        cost_estimate=pl.CostEstimate(
            flops=2 * 5 * C * C * 8192, bytes_accessed=8 << 20, transcendentals=2 << 20
        ),
        name="edges",
    )(pair4, lg, lp, rg, rp, og)


def turn(top, low):
    h = top.shape[1] // 2
    return (
        jnp.concatenate([top[:, :h], low[:, :h]], axis=1),
        jnp.concatenate([top[:, h:], low[:, h:]], axis=1),
    )


def mix_kernel(got_ref, o_ref, left, right):
    rows, cols, _, s, _ = got_ref.shape
    for side, dst in enumerate((left, right)):
        for r in range(rows):
            for q in range(0, cols, 2):
                a, b = turn(got_ref[r, q, side], got_ref[r, q + 1, side])
                dst[2 * r * s : 2 * r * s + s, q * s : q * s + 2 * s] = a
                dst[2 * r * s + s : 2 * r * s + 2 * s, q * s : q * s + 2 * s] = b
    wide = 4
    for n in range(0, cols, wide):
        m = lax.dot_general(
            left[...], right[n * s : (n + wide) * s, :], NT, preferred_element_type=F32
        ).astype(BF16)
        for r in range(rows):
            top = m[2 * r * s : 2 * r * s + s]
            low = m[2 * r * s + s : 2 * r * s + 2 * s]
            for q in range(0, wide, 2):
                at = slice(q * s, q * s + 2 * s)
                a, b = turn(top[:, at], low[:, at])
                o_ref[r, n + q] = a
                o_ref[r, n + q + 1] = b


def mix(got, rows, cols):
    steps, lanes = got.shape[2], got.shape[3]
    got = got.reshape(rows, cols, 2, steps, lanes)
    edge = pltpu.VMEM((2 * rows * steps, cols * steps), BF16)
    return pl.pallas_call(
        mix_kernel,
        in_specs=[pl.BlockSpec(memory_space=pltpu.VMEM)],
        out_specs=pl.BlockSpec(memory_space=pltpu.VMEM),
        out_shape=jax.ShapeDtypeStruct((rows, cols, steps, lanes), BF16),
        scratch_shapes=[edge, edge],
        compiler_params=pltpu.CompilerParams(vmem_limit_bytes=VMEM),
        cost_estimate=pl.CostEstimate(
            flops=2 << 30, bytes_accessed=6 << 20, transcendentals=0
        ),
        name="mix",
    )(got).reshape(rows * cols, steps, lanes)


def tree_sum(term):
    sums = [term(c) for c in range(4)]
    for c in range(4, C):
        sums[c % 4] += term(c)
    return (sums[0] + sums[1]) + (sums[2] + sums[3])


def update_kernel(
    m_ref, g_ref, w_ref, o_hbm, stage, o_ref, o_sem
):
    parts = o_sem.shape[0]
    part = o_ref.shape[1] // parts
    cols = o_ref.shape[2]
    stores = []
    for n in range(parts):
        first = n * part

        def channel(c):
            return m_ref[c, first : first + part, :].astype(F32)

        mean = tree_sum(channel) * (1 / C)
        spread = tree_sum(lambda c: jnp.square(channel(c) - mean)) * (1 / C)
        scale = lax.rsqrt(spread + 1e-05)
        for c in range(C):
            stage[c * PITCH : c * PITCH + part, :] = (channel(c) - mean) * scale
        for s in range(part):
            x = stage[pl.ds(s, C, stride=PITCH), :].astype(BF16)
            p = lax.dot_general(x, w_ref[...], TN, preferred_element_type=F32)
            o_ref[0, first + s] = (p[:cols] * g_ref[0, first + s]).astype(BF16)
            o_ref[1, first + s] = (p[cols:] * g_ref[1, first + s]).astype(BF16)
        at = pl.ds(first, part)
        store = pltpu.make_async_copy(o_ref.at[:, at], o_hbm.at[:, at], o_sem.at[n])
        store.start()
        stores.append(store)
    for store in stores:
        store.wait()


def update(mixed, gate4, w):
    _, steps, cols, ch = gate4.shape
    parts = steps // BLOCK
    hbm = pl.BlockSpec(memory_space=pltpu.HBM)
    sems = pltpu.SemaphoreType.DMA((parts,))
    return pl.pallas_call(
        update_kernel,
        in_specs=[pl.BlockSpec(memory_space=pltpu.VMEM)] * 3,
        out_specs=hbm,
        out_shape=jax.ShapeDtypeStruct(gate4.shape, BF16),
        scratch_shapes=[
            pltpu.VMEM((C * PITCH, 2 * cols), F32),
            pltpu.VMEM(gate4.shape, BF16),
            sems,
        ],
        compiler_params=pltpu.CompilerParams(vmem_limit_bytes=VMEM),
        cost_estimate=pl.CostEstimate(
            flops=2 * C * C * 8192, bytes_accessed=8 << 20, transcendentals=0
        ),
        name="update",
    )(mixed, gate4, w)


def on_device(rows, cols, pair, left_gate, left_proj, right_gate, right_proj, out_gate, out_proj):
    ni, nj, ch = pair.shape
    pair4 = pair.reshape(2, ni // 2, nj, ch)
    sent, gate = edges(pair4, left_gate, left_proj, right_gate, right_proj, out_gate)
    got = lax.all_to_all(sent, ("row", "col"), 0, 0, tiled=True)
    mixed = mix(got, rows, cols)
    mixed = lax.all_to_all(mixed, ("row", "col"), 0, 0, tiled=True)
    out = update(mixed, gate, out_proj)
    return out.reshape(ni, nj, ch)


def solution(mesh):
    rows, cols = mesh.shape["row"], mesh.shape["col"]

    def body(*args):
        return on_device(rows, cols, *args)

    return jax.shard_map(
        body,
        mesh=mesh,
        in_specs=(P("row", "col", None), P(), P(), P(), P(), P(), P()),
        out_specs=P("row", "col", None),
        check_vma=False,
    )
```

profile of v0, /device:TPU:1, one launch (start us, length us, event | category | flops | bytes accessed | tf_op | source)
XLA Modules:
  0.0 112.4 jit_solution(6734073803224689994)
XLA Ops:
  0.0 7.3 %edges.1 = (bf16[128,2,64,128]{3,2,1,0:T(8,128)(2,1)}, bf16[2,64,64,128]{3,2,1,0:T(8,128)(2,1)}) custom-call(bf16[2,64,64,128]{3,2,1,0:T(8,128)(2,1)} %bitcast.6, bf16[128,128]{1,0:T(8,128)(2,1)} %lg_hbm.1, bf16[128,128]{1,0:T(8,128)(2,1)} %lp_hbm.1, bf16[128,128]{1,0:T(8,128)(2,1)} %rg_hbm.1, bf16[128,128]{1,0:T(8,128)(2,1)} %rp_hbm.1, bf16[128,128]{1,0:T(8,128)(2,1)} %og_hbm.1), custom_call_target="tpu_custom_call" | custom-call | flops 1342177280 | bytes 8388608 | tf_op jit(solution)/shard_map/edges/pallas_call | solution.py:95
  7.3 64.7 %all_to_all.10 = bf16[128,2,64,128]{3,2,1,0:T(8,128)(2,1)S(1)} all-to-all(bf16[128,2,64,128]{3,2,1,0:T(8,128)(2,1)} %get-tuple-element.7), channel_id=1, replica_groups=mesh['row'=8,'col'=16] {'row','col'}, dimensions={0} | all-to-all | bytes 8388608 | tf_op jit(solution)/shard_map/all_to_all | solution.py:238
  72.0 2.6 %mix.1 = bf16[8,16,64,128]{3,2,1,0:T(8,128)(2,1)S(1)} custom-call(bf16[8,16,2,64,128]{4,3,2,1,0:T(8,128)(2,1)S(1)} %bitcast.4), custom_call_target="tpu_custom_call" | custom-call | flops 2147483648 | bytes 6291456 | tf_op jit(solution)/shard_map/mix/pallas_call | solution.py:159
  74.6 0.0 copy-start
  74.6 0.0 copy-start.1
  74.6 34.4 %all_to_all.11.m_ref = bf16[128,64,128]{2,1,0:T(8,128)(2,1)S(1)} all-to-all(bf16[128,64,128]{2,1,0:T(8,128)(2,1)S(1)} %bitcast.5), channel_id=1, replica_groups=mesh['row'=8,'col'=16] {'row','col'}, dimensions={0} | all-to-all | bytes 4194304 | tf_op jit(solution)/shard_map/all_to_all | solution.py:240
  109.0 0.0 copy-done
  109.0 0.0 copy-done.1
  109.0 3.4 %update.1 = bf16[2,64,64,128]{3,2,1,0:T(8,128)(2,1)} custom-call(bf16[128,64,128]{2,1,0:T(8,128)(2,1)S(1)} %all_to_all.11.m_ref, bf16[2,64,64,128]{3,2,1,0:T(8,128)(2,1)S(1)} %copy-done, bf16[128,128]{1,0:T(8,128)(2,1)S(1)} %copy-done.1), custom_call_target="tpu_custom_call" | custom-call | flops 268435456 | bytes 8388608 | tf_op jit(solution)/shard_map/update/pallas_call | solution.py:216
Async XLA Ops:
  74.6 34.4 %copy-start = (bf16[2,64,64,128]{3,2,1,0:T(8,128)(2,1)S(1)}, bf16[2,64,64,128]{3,2,1,0:T(8,128)(2,1)}, u32[]{:S(2)}) copy-start(bf16[2,64,64,128]{3,2,1,0:T(8,128)(2,1)} %get-tuple-element.8.g_ref) | copy-start | bytes 6291460
  74.6 34.4 %copy-start.1 = (bf16[128,128]{1,0:T(8,128)(2,1)S(1)}, bf16[128,128]{1,0:T(8,128)(2,1)}, u32[]{:S(2)}) copy-start(bf16[128,128]{1,0:T(8,128)(2,1)} %w_ref.1) | copy-start | bytes 98308
where the time goes:
time: 113 us; the launch traced here: 112 us
  blocking collectives  99.1 us (88%)
  Pallas kernels  13.3 us (12%)
    all_to_all x1, blocking collectives, on_device(): got = lax.all_to_all(sent, ('row', 'col'), 0, 0, tiled=True)  64.7 us
    all_to_all x1, blocking collectives, on_device(): mixed = lax.all_to_all(mixed, ('row', 'col'), 0, 0, tiled=True)  34.4 us
    pallas_call x1, Pallas kernels, edges(): pl.pallas_call(edges_kernel, in_specs=[hbm] * 6, out_specs=[hbm, hbm], ou...  7.29 us
    pallas_call x1, Pallas kernels, update(): pl.pallas_call(update_kernel, in_specs=[pl.BlockSpec(memory_space=pltpu.V...  3.37 us
    pallas_call x1, Pallas kernels, mix(): pl.pallas_call(mix_kernel, in_specs=[pl.BlockSpec(memory_space=pltpu.VMEM...  2.61 us

commit v1 on v0

--- a/solution.py
+++ b/solution.py
@@ -1,5 +1,8 @@
+import functools
+
 import jax
 import jax.numpy as jnp
+import numpy as np
 from jax import lax
 from jax.experimental import pallas as pl
 from jax.experimental.pallas import tpu as pltpu
@@ -49,9 +52,10 @@
         else:
             w_in[n] = w_in[n] * 0.5
 
+    for copy in loads:
+        copy.wait()
     stores = []
-    for n, copy in enumerate(loads):
-        copy.wait()
+    for n in range(parts):
         first = n * part
         for s in range(0, part, 2):
             x = jnp.concatenate(
@@ -129,12 +133,13 @@
     )
 
 
-def mix_kernel(got_ref, o_ref, left, right):
-    rows, cols, _, s, _ = got_ref.shape
+def mix_kernel(source, target, got_ref, o_ref, left, right):
+    rows, cols = source.shape
+    s = got_ref.shape[2]
     for side, dst in enumerate((left, right)):
         for r in range(rows):
             for q in range(0, cols, 2):
-                a, b = turn(got_ref[r, q, side], got_ref[r, q + 1, side])
+                a, b = turn(got_ref[source[r, q], side], got_ref[source[r, q + 1], side])
                 dst[2 * r * s : 2 * r * s + s, q * s : q * s + 2 * s] = a
                 dst[2 * r * s + s : 2 * r * s + 2 * s, q * s : q * s + 2 * s] = b
     wide = 4
@@ -148,26 +153,26 @@
             for q in range(0, wide, 2):
                 at = slice(q * s, q * s + 2 * s)
                 a, b = turn(top[:, at], low[:, at])
-                o_ref[r, n + q] = a
-                o_ref[r, n + q + 1] = b
-
-
-def mix(got, rows, cols):
-    steps, lanes = got.shape[2], got.shape[3]
-    got = got.reshape(rows, cols, 2, steps, lanes)
+                o_ref[target[r, n + q]] = a
+                o_ref[target[r, n + q + 1]] = b
+
+
+def mix(got, source, target):
+    count, _, steps, lanes = got.shape
+    rows, cols = source.shape
     edge = pltpu.VMEM((2 * rows * steps, cols * steps), BF16)
     return pl.pallas_call(
-        mix_kernel,
+        functools.partial(mix_kernel, source, target),
         in_specs=[pl.BlockSpec(memory_space=pltpu.VMEM)],
         out_specs=pl.BlockSpec(memory_space=pltpu.VMEM),
-        out_shape=jax.ShapeDtypeStruct((rows, cols, steps, lanes), BF16),
+        out_shape=jax.ShapeDtypeStruct((count, steps, lanes), BF16),
         scratch_shapes=[edge, edge],
         compiler_params=pltpu.CompilerParams(vmem_limit_bytes=VMEM),
         cost_estimate=pl.CostEstimate(
             flops=2 << 30, bytes_accessed=6 << 20, transcendentals=0
         ),
         name="mix",
-    )(got).reshape(rows * cols, steps, lanes)
+    )(got)
 
 
 def tree_sum(term):
@@ -178,7 +183,7 @@
 
 
 def update_kernel(
-    m_ref, g_ref, w_ref, o_hbm, stage, o_ref, o_sem
+    holder, m_ref, g_ref, w_ref, o_hbm, stage, o_ref, o_sem
 ):
     parts = o_sem.shape[0]
     part = o_ref.shape[1] // parts
@@ -188,7 +193,7 @@
         first = n * part
 
         def channel(c):
-            return m_ref[c, first : first + part, :].astype(F32)
+            return m_ref[holder[c], first : first + part, :].astype(F32)
 
         mean = tree_sum(channel) * (1 / C)
         spread = tree_sum(lambda c: jnp.square(channel(c) - mean)) * (1 / C)
@@ -208,13 +213,13 @@
         store.wait()
 
 
-def update(mixed, gate4, w):
+def update(mixed, gate4, w, holder):
     _, steps, cols, ch = gate4.shape
     parts = steps // BLOCK
     hbm = pl.BlockSpec(memory_space=pltpu.HBM)
     sems = pltpu.SemaphoreType.DMA((parts,))
     return pl.pallas_call(
-        update_kernel,
+        functools.partial(update_kernel, holder),
         in_specs=[pl.BlockSpec(memory_space=pltpu.VMEM)] * 3,
         out_specs=hbm,
         out_shape=jax.ShapeDtypeStruct(gate4.shape, BF16),
@@ -231,27 +236,38 @@
     )(mixed, gate4, w)
 
 
-def on_device(rows, cols, pair, left_gate, left_proj, right_gate, right_proj, out_gate, out_proj):
+FIRST = ("xl", "xh", "y", "core", "z")
+SECOND = ("core", "y", "xl", "xh", "z")
+SIZES = {"z": 4, "xh": 2, "xl": 2, "y": 4, "core": 2}
+AXES = tuple(SIZES)
+
+
+def places(order):
+    counts = np.arange(128).reshape([SIZES[axis] for axis in order])
+    return counts.transpose([order.index(axis) for axis in AXES]).reshape(8, 16)
+
+
+def on_device(pair, left_gate, left_proj, right_gate, right_proj, out_gate, out_proj):
+    first, second = places(FIRST), places(SECOND)
+    holder = np.empty(128, int)
+    holder[first.reshape(-1)] = second.reshape(-1)
     ni, nj, ch = pair.shape
     pair4 = pair.reshape(2, ni // 2, nj, ch)
     sent, gate = edges(pair4, left_gate, left_proj, right_gate, right_proj, out_gate)
-    got = lax.all_to_all(sent, ("row", "col"), 0, 0, tiled=True)
-    mixed = mix(got, rows, cols)
-    mixed = lax.all_to_all(mixed, ("row", "col"), 0, 0, tiled=True)
-    out = update(mixed, gate, out_proj)
+    got = lax.all_to_all(sent, FIRST, 0, 0, tiled=True)
+    mixed = mix(got, first, second)
+    mixed = lax.all_to_all(mixed, SECOND, 0, 0, tiled=True)
+    out = update(mixed, gate, out_proj, holder)
     return out.reshape(ni, nj, ch)
 
 
 def solution(mesh):
-    rows, cols = mesh.shape["row"], mesh.shape["col"]
-
-    def body(*args):
-        return on_device(rows, cols, *args)
-
+    split = jax.sharding.Mesh(mesh.devices.reshape(tuple(SIZES.values())), AXES)
+    spec = P(("z", "xh"), ("xl", "y", "core"), None)
     return jax.shard_map(
-        body,
-        mesh=mesh,
-        in_specs=(P("row", "col", None), P(), P(), P(), P(), P(), P()),
-        out_specs=P("row", "col", None),
+        on_device,
+        mesh=split,
+        in_specs=(spec, P(), P(), P(), P(), P(), P()),
+        out_specs=spec,
         check_vma=False,
     )

time: 113 us -> 111 us (0.982)
  blocking collectives: 99.1 us -> 97.8 us
    all_to_all x2, blocking collectives: 99.1 us -> 97.8 us  [the longest x1 63.6 us: on_device(): got = lax.all_to_all(sent, FIRST, 0, 0, tiled=True)]
where the time goes in v1:
time: 111 us
  blocking collectives  97.8 us (88%)
  Pallas kernels  12.8 us (12%)
    all_to_all x1, blocking collectives, on_device(): got = lax.all_to_all(sent, FIRST, 0, 0, tiled=True)  63.6 us
    all_to_all x1, blocking collectives, on_device(): mixed = lax.all_to_all(mixed, SECOND, 0, 0, tiled=True)  34.2 us
    pallas_call x1, Pallas kernels, edges(): pl.pallas_call(edges_kernel, in_specs=[hbm] * 6, out_specs=[hbm, hbm], ou...  6.84 us
    pallas_call x1, Pallas kernels, update(): pl.pallas_call(functools.partial(update_kernel, holder), in_specs=[pl.Blo...  3.37 us
    pallas_call x1, Pallas kernels, mix(): pl.pallas_call(functools.partial(mix_kernel, source, target), in_specs=[p...  2.61 us

profile of v1, /device:TPU:1, one launch (start us, length us, event | category | flops | bytes accessed | tf_op | source)
XLA Modules:
  0.0 110.7 jit_solution(11862441443442379663)
XLA Ops:
  0.0 6.8 %edges.1 = (bf16[128,2,64,128]{3,2,1,0:T(8,128)(2,1)}, bf16[2,64,64,128]{3,2,1,0:T(8,128)(2,1)}) custom-call(bf16[2,64,64,128]{3,2,1,0:T(8,128)(2,1)} %bitcast.2, bf16[128,128]{1,0:T(8,128)(2,1)} %lg_hbm.1, bf16[128,128]{1,0:T(8,128)(2,1)} %lp_hbm.1, bf16[128,128]{1,0:T(8,128)(2,1)} %rg_hbm.1, bf16[128,128]{1,0:T(8,128)(2,1)} %rp_hbm.1, bf16[128,128]{1,0:T(8,128)(2,1)} %og_hbm.1), custom_call_target="tpu_custom_call" | custom-call | flops 1342177280 | bytes 8388608 | tf_op jit(solution)/shard_map/edges/pallas_call | solution.py:99
  6.8 63.6 %all_to_all.10.got_ref = bf16[128,2,64,128]{3,2,1,0:T(8,128)(2,1)S(1)} all-to-all(bf16[128,2,64,128]{3,2,1,0:T(8,128)(2,1)} %get-tuple-element.7), channel_id=1, replica_groups=mesh['z'=4,'xh'=2,'xl'=2,'y'=4,'core'=2] {'xl','xh','y','core','z'}, dimensions={0} | all-to-all | bytes 8388608 | tf_op jit(solution)/shard_map/all_to_all | solution.py:257
  70.5 2.6 %mix.1 = bf16[128,64,128]{2,1,0:T(8,128)(2,1)S(1)} custom-call(bf16[128,2,64,128]{3,2,1,0:T(8,128)(2,1)S(1)} %all_to_all.10.got_ref), custom_call_target="tpu_custom_call" | custom-call | flops 2147483648 | bytes 6291456 | tf_op jit(solution)/shard_map/mix/pallas_call | solution.py:164
  73.1 0.0 copy-start
  73.1 0.0 copy-start.1
  73.1 34.2 %all_to_all.11.m_ref = bf16[128,64,128]{2,1,0:T(8,128)(2,1)S(1)} all-to-all(bf16[128,64,128]{2,1,0:T(8,128)(2,1)S(1)} %mix.1), channel_id=1, replica_groups=mesh['z'=4,'xh'=2,'xl'=2,'y'=4,'core'=2] {'core','y','xl','xh','z'}, dimensions={0} | all-to-all | bytes 4194304 | tf_op jit(solution)/shard_map/all_to_all | solution.py:259
  107.3 0.0 copy-done
  107.3 0.0 copy-done.1
  107.3 3.4 %update.1 = bf16[2,64,64,128]{3,2,1,0:T(8,128)(2,1)} custom-call(bf16[128,64,128]{2,1,0:T(8,128)(2,1)S(1)} %all_to_all.11.m_ref, bf16[2,64,64,128]{3,2,1,0:T(8,128)(2,1)S(1)} %copy-done, bf16[128,128]{1,0:T(8,128)(2,1)S(1)} %copy-done.1), custom_call_target="tpu_custom_call" | custom-call | flops 268435456 | bytes 8388608 | tf_op jit(solution)/shard_map/update/pallas_call | solution.py:221
Async XLA Ops:
  73.1 34.2 %copy-start = (bf16[2,64,64,128]{3,2,1,0:T(8,128)(2,1)S(1)}, bf16[2,64,64,128]{3,2,1,0:T(8,128)(2,1)}, u32[]{:S(2)}) copy-start(bf16[2,64,64,128]{3,2,1,0:T(8,128)(2,1)} %get-tuple-element.8.g_ref) | copy-start | bytes 6291460
  73.1 34.2 %copy-start.1 = (bf16[128,128]{1,0:T(8,128)(2,1)S(1)}, bf16[128,128]{1,0:T(8,128)(2,1)}, u32[]{:S(2)}) copy-start(bf16[128,128]{1,0:T(8,128)(2,1)} %w_ref.1) | copy-start | bytes 98308

commit v2 on v1

--- a/solution.py
+++ b/solution.py
@@ -236,8 +236,8 @@
     )(mixed, gate4, w)
 
 
-FIRST = ("xl", "xh", "y", "core", "z")
-SECOND = ("core", "y", "xl", "xh", "z")
+FIRST = ("z", "xl", "xh", "core", "y")
+SECOND = ("core", "y", "xh", "xl", "z")
 SIZES = {"z": 4, "xh": 2, "xl": 2, "y": 4, "core": 2}
 AXES = tuple(SIZES)
 

time: 111 us -> 110 us (level)
    all_to_all x1, blocking collectives: 34.2 us -> 32.5 us  [on_device(): mixed = lax.all_to_all(mixed, SECOND, 0, 0, tiled=True)]
where the time goes in v2:
time: 110 us
  blocking collectives  97.2 us (88%)
  Pallas kernels  12.9 us (12%)
    all_to_all x1, blocking collectives, on_device(): got = lax.all_to_all(sent, FIRST, 0, 0, tiled=True)  64.7 us
    all_to_all x1, blocking collectives, on_device(): mixed = lax.all_to_all(mixed, SECOND, 0, 0, tiled=True)  32.5 us
    pallas_call x1, Pallas kernels, edges(): pl.pallas_call(edges_kernel, in_specs=[hbm] * 6, out_specs=[hbm, hbm], ou...  6.84 us
    pallas_call x1, Pallas kernels, update(): pl.pallas_call(functools.partial(update_kernel, holder), in_specs=[pl.Blo...  3.41 us
    pallas_call x1, Pallas kernels, mix(): pl.pallas_call(functools.partial(mix_kernel, source, target), in_specs=[p...  2.61 us

profile of v2, /device:TPU:1, one launch (start us, length us, event | category | flops | bytes accessed | tf_op | source)
XLA Modules:
  0.0 110.1 jit_solution(5574111483585460281)
XLA Ops:
  0.0 6.8 %edges.1 = (bf16[128,2,64,128]{3,2,1,0:T(8,128)(2,1)}, bf16[2,64,64,128]{3,2,1,0:T(8,128)(2,1)}) custom-call(bf16[2,64,64,128]{3,2,1,0:T(8,128)(2,1)} %bitcast.2, bf16[128,128]{1,0:T(8,128)(2,1)} %lg_hbm.1, bf16[128,128]{1,0:T(8,128)(2,1)} %lp_hbm.1, bf16[128,128]{1,0:T(8,128)(2,1)} %rg_hbm.1, bf16[128,128]{1,0:T(8,128)(2,1)} %rp_hbm.1, bf16[128,128]{1,0:T(8,128)(2,1)} %og_hbm.1), custom_call_target="tpu_custom_call" | custom-call | flops 1342177280 | bytes 8388608 | tf_op jit(solution)/shard_map/edges/pallas_call | solution.py:99
  6.8 64.7 %all_to_all.10.got_ref = bf16[128,2,64,128]{3,2,1,0:T(8,128)(2,1)S(1)} all-to-all(bf16[128,2,64,128]{3,2,1,0:T(8,128)(2,1)} %get-tuple-element.7), channel_id=1, replica_groups=mesh['z'=4,'xh'=2,'xl'=2,'y'=4,'core'=2] {'z','xl','xh','core','y'}, dimensions={0} | all-to-all | bytes 8388608 | tf_op jit(solution)/shard_map/all_to_all | solution.py:257
  71.6 2.6 %mix.1 = bf16[128,64,128]{2,1,0:T(8,128)(2,1)S(1)} custom-call(bf16[128,2,64,128]{3,2,1,0:T(8,128)(2,1)S(1)} %all_to_all.10.got_ref), custom_call_target="tpu_custom_call" | custom-call | flops 2147483648 | bytes 6291456 | tf_op jit(solution)/shard_map/mix/pallas_call | solution.py:164
  74.2 0.0 copy-start
  74.2 0.0 copy-start.1
  74.2 32.5 %all_to_all.11.m_ref = bf16[128,64,128]{2,1,0:T(8,128)(2,1)S(1)} all-to-all(bf16[128,64,128]{2,1,0:T(8,128)(2,1)S(1)} %mix.1), channel_id=1, replica_groups=mesh['z'=4,'xh'=2,'xl'=2,'y'=4,'core'=2] {'core','y','xh','xl','z'}, dimensions={0} | all-to-all | bytes 4194304 | tf_op jit(solution)/shard_map/all_to_all | solution.py:259
  106.7 0.0 copy-done
  106.7 0.0 copy-done.1
  106.7 3.4 %update.1 = bf16[2,64,64,128]{3,2,1,0:T(8,128)(2,1)} custom-call(bf16[128,64,128]{2,1,0:T(8,128)(2,1)S(1)} %all_to_all.11.m_ref, bf16[2,64,64,128]{3,2,1,0:T(8,128)(2,1)S(1)} %copy-done, bf16[128,128]{1,0:T(8,128)(2,1)S(1)} %copy-done.1), custom_call_target="tpu_custom_call" | custom-call | flops 268435456 | bytes 8388608 | tf_op jit(solution)/shard_map/update/pallas_call | solution.py:221
Async XLA Ops:
  74.2 32.5 %copy-start = (bf16[2,64,64,128]{3,2,1,0:T(8,128)(2,1)S(1)}, bf16[2,64,64,128]{3,2,1,0:T(8,128)(2,1)}, u32[]{:S(2)}) copy-start(bf16[2,64,64,128]{3,2,1,0:T(8,128)(2,1)} %get-tuple-element.8.g_ref) | copy-start | bytes 6291460
  74.2 32.5 %copy-start.1 = (bf16[128,128]{1,0:T(8,128)(2,1)S(1)}, bf16[128,128]{1,0:T(8,128)(2,1)}, u32[]{:S(2)}) copy-start(bf16[128,128]{1,0:T(8,128)(2,1)} %w_ref.1) | copy-start | bytes 98308

commit v3 on v2

--- a/solution.py
+++ b/solution.py
@@ -236,7 +236,7 @@
     )(mixed, gate4, w)
 
 
-FIRST = ("z", "xl", "xh", "core", "y")
+FIRST = ("core", "y", "xh", "xl", "z")
 SECOND = ("core", "y", "xh", "xl", "z")
 SIZES = {"z": 4, "xh": 2, "xl": 2, "y": 4, "core": 2}
 AXES = tuple(SIZES)

time: 110 us -> 116 us (1.055)
  blocking collectives: 97.2 us -> 103 us
    all_to_all x1, blocking collectives: 32.5 us -> 39.4 us  [on_device(): mixed = lax.all_to_all(mixed, SECOND, 0, 0, tiled=True)]
    all_to_all x1, blocking collectives: 64.7 us -> 63.1 us  [on_device(): got = lax.all_to_all(sent, FIRST, 0, 0, tiled=True)]
where the time goes in v3:
time: 116 us; the launch traced here: 115 us
  blocking collectives  103 us (89%)
  Pallas kernels  12.8 us (11%)
    all_to_all x1, blocking collectives, on_device(): got = lax.all_to_all(sent, FIRST, 0, 0, tiled=True)  63.1 us
    all_to_all x1, blocking collectives, on_device(): mixed = lax.all_to_all(mixed, SECOND, 0, 0, tiled=True)  39.4 us
    pallas_call x1, Pallas kernels, edges(): pl.pallas_call(edges_kernel, in_specs=[hbm] * 6, out_specs=[hbm, hbm], ou...  6.84 us
    pallas_call x1, Pallas kernels, update(): pl.pallas_call(functools.partial(update_kernel, holder), in_specs=[pl.Blo...  3.37 us
    pallas_call x1, Pallas kernels, mix(): pl.pallas_call(functools.partial(mix_kernel, source, target), in_specs=[p...  2.61 us

profile of v3, /device:TPU:1, one launch (start us, length us, event | category | flops | bytes accessed | tf_op | source)
XLA Modules:
  0.0 115.4 jit_solution(682625640398254957)
XLA Ops:
  0.0 6.8 %edges.1 = (bf16[128,2,64,128]{3,2,1,0:T(8,128)(2,1)}, bf16[2,64,64,128]{3,2,1,0:T(8,128)(2,1)}) custom-call(bf16[2,64,64,128]{3,2,1,0:T(8,128)(2,1)} %bitcast.2, bf16[128,128]{1,0:T(8,128)(2,1)} %lg_hbm.1, bf16[128,128]{1,0:T(8,128)(2,1)} %lp_hbm.1, bf16[128,128]{1,0:T(8,128)(2,1)} %rg_hbm.1, bf16[128,128]{1,0:T(8,128)(2,1)} %rp_hbm.1, bf16[128,128]{1,0:T(8,128)(2,1)} %og_hbm.1), custom_call_target="tpu_custom_call" | custom-call | flops 1342177280 | bytes 8388608 | tf_op jit(solution)/shard_map/edges/pallas_call | solution.py:99
  6.8 63.1 %all_to_all.10.got_ref = bf16[128,2,64,128]{3,2,1,0:T(8,128)(2,1)S(1)} all-to-all(bf16[128,2,64,128]{3,2,1,0:T(8,128)(2,1)} %get-tuple-element.7), channel_id=1, replica_groups=mesh['z'=4,'xh'=2,'xl'=2,'y'=4,'core'=2] {'core','y','xh','xl','z'}, dimensions={0} | all-to-all | bytes 8388608 | tf_op jit(solution)/shard_map/all_to_all | solution.py:257
  69.9 2.6 %mix.1 = bf16[128,64,128]{2,1,0:T(8,128)(2,1)S(1)} custom-call(bf16[128,2,64,128]{3,2,1,0:T(8,128)(2,1)S(1)} %all_to_all.10.got_ref), custom_call_target="tpu_custom_call" | custom-call | flops 2147483648 | bytes 6291456 | tf_op jit(solution)/shard_map/mix/pallas_call | solution.py:164
  72.6 0.0 copy-start
  72.6 0.0 copy-start.1
  72.6 39.4 %all_to_all.11.m_ref = bf16[128,64,128]{2,1,0:T(8,128)(2,1)S(1)} all-to-all(bf16[128,64,128]{2,1,0:T(8,128)(2,1)S(1)} %mix.1), channel_id=1, replica_groups=mesh['z'=4,'xh'=2,'xl'=2,'y'=4,'core'=2] {'core','y','xh','xl','z'}, dimensions={0} | all-to-all | bytes 4194304 | tf_op jit(solution)/shard_map/all_to_all | solution.py:259
  112.0 0.0 copy-done
  112.0 0.0 copy-done.1
  112.0 3.4 %update.1 = bf16[2,64,64,128]{3,2,1,0:T(8,128)(2,1)} custom-call(bf16[128,64,128]{2,1,0:T(8,128)(2,1)S(1)} %all_to_all.11.m_ref, bf16[2,64,64,128]{3,2,1,0:T(8,128)(2,1)S(1)} %copy-done, bf16[128,128]{1,0:T(8,128)(2,1)S(1)} %copy-done.1), custom_call_target="tpu_custom_call" | custom-call | flops 268435456 | bytes 8388608 | tf_op jit(solution)/shard_map/update/pallas_call | solution.py:221
Async XLA Ops:
  72.6 39.4 %copy-start = (bf16[2,64,64,128]{3,2,1,0:T(8,128)(2,1)S(1)}, bf16[2,64,64,128]{3,2,1,0:T(8,128)(2,1)}, u32[]{:S(2)}) copy-start(bf16[2,64,64,128]{3,2,1,0:T(8,128)(2,1)} %get-tuple-element.8.g_ref) | copy-start | bytes 6291460
  72.6 39.4 %copy-start.1 = (bf16[128,128]{1,0:T(8,128)(2,1)S(1)}, bf16[128,128]{1,0:T(8,128)(2,1)}, u32[]{:S(2)}) copy-start(bf16[128,128]{1,0:T(8,128)(2,1)} %w_ref.1) | copy-start | bytes 98308
